TPU v7x, 32 devices: a whole 2x2x4 slice. The times are simulated.
32 devices in a mesh: space: 8 (over z, x), member: 4 (over y, core).
Axes of the slice: x: 2, y: 2, z: 4, core: 2. Of those that a mesh axis runs over, the one named last changes fastest.
Arguments:
- state: float32 [32, 49152], P(None, 'space'), may hold values from -6 to 6
- ensemble: bfloat16 [4, 32, 49152], P('member', None, 'space'), may hold values from -6 to 6
- vertical: bfloat16 [32, 32], replicated, may hold values from -1 to 1
- coords: int32 [2, 49152], P(None, 'space'), may hold values from 0 to 6143, as said below
- pairs: int32 [2, 1920], P(None, 'space'), may hold values from 0 to 51, as said below
- pair_count: int32 [8], P('space'), may hold values from 60 to 240, as said below
Outputs:
- first: float32 [32, 49152], P(None, 'space')
- second: float32 [32, 49152], P(None, 'space')
Inputs may be any that keep to these rules, and one draw needn't show every extreme that they name: `coords`: row 0 is a position on a periodic strip of 6144 positions: column g lies 0 to 47 positions ahead of g // 8, periodically; row 1 lies in 0 to 31. Each tile's 240 slots hold distinct pairs; the destination is 0 to 47 and the source lies from the destination to the destination + 4. Only the first pair_count[t] slots of tile t are live.
All inputs are finite; a program needn't handle non-finite values.
Results may differ from a plain program's by a relative error of at most 0.0057.
Values may be sent and summed in bfloat16 or wider, within the bound.
A program may use at most 64 MiB of HBM per device.

v0:
```python
import jax
import jax.numpy as jnp
from jax import lax
from jax.sharding import PartitionSpec as P

BLOCK = 128
REACH = 2


scale_len = 4.0


def extended(block, sides, width):
    for axis, dim in sides:
        count = lax.axis_size(axis)
        forward = [(i, i + 1) for i in range(count - 1)]
        forward.append((count - 1, 0))
        backward = [(target, source) for source, target in forward]
        low = lax.ppermute(
            lax.slice_in_dim(block, block.shape[dim] - width, None, axis=dim), axis, forward
        )
        high = lax.ppermute(lax.slice_in_dim(block, 0, width, axis=dim), axis, backward)
        block = jnp.concatenate([low, block, high], axis=dim)
    return block


def gaspari(r):
    near = (((-0.25 * r + 0.5) * r + 0.625) * r - 5.0 / 3.0) * r * r + 1.0
    rf = jnp.maximum(r, 1.0)
    far = (
        ((((rf / 12.0 - 0.5) * rf + 0.625) * rf + 5.0 / 3.0) * rf - 5.0) * rf
        + 4.0
        - 2.0 / (3.0 * rf)
    )
    return jnp.where(r <= 1.0, near, jnp.where(r < 2.0, far, jnp.zeros_like(r)))


def pair_weights(src_xy, dst_xy, period):
    along = jnp.abs(src_xy[0][:, :, None] - dst_xy[0][:, None, :])
    along = jnp.minimum(along, period - along)
    across = jnp.abs(src_xy[1][:, :, None] - dst_xy[1][:, None, :])
    dist = jnp.sqrt((along * along + across * across).astype(jnp.float32))
    return gaspari(dist / scale_len).astype(jnp.bfloat16)


def stacked_windows(blocks, blocks_dev, span):
    return jnp.concatenate(
        [blocks[..., offset : offset + blocks_dev, :] for offset in range(span)], axis=-1
    )


def on_device(state, ensemble, vertical, coords, pairs, pair_count):
    tiles = lax.axis_size("space")
    members = lax.axis_size("member")
    cols_dev = state.shape[1]
    blocks_dev = cols_dev // BLOCK
    slots = pairs.shape[1]
    span = 2 * REACH + 1
    period = cols_dev * tiles // 8
    xy_ext = extended(coords, (("space", 1),), REACH * BLOCK)
    src_xy = stacked_windows(xy_ext.reshape(2, -1, BLOCK), blocks_dev, span)
    dst_xy = coords.reshape(2, blocks_dev, BLOCK)
    target = pairs[0]
    offset_of = pairs[1] - target
    live = jnp.arange(slots, dtype=jnp.int32) < pair_count[0]
    code_of = target * span + offset_of
    hits = (code_of[:, None] == jnp.arange(blocks_dev * span, dtype=jnp.int32)[None, :]) & live[
        :, None
    ]
    present = jnp.any(hits, axis=0).reshape(blocks_dev, span)
    dense = pair_weights(src_xy, dst_xy, period).reshape(blocks_dev, span, BLOCK, BLOCK)
    dense = dense * present[:, :, None, None].astype(jnp.bfloat16)
    own = ensemble[0]

    def horizontal(lifted):
        ext = extended(lifted, (("space", 1),), REACH * BLOCK)
        height = ext.shape[0]
        blocks = ext.reshape(height, -1, BLOCK)
        windows = stacked_windows(blocks, blocks_dev, span)
        spread = jnp.einsum(
            "hno,nos->hns",
            windows,
            dense.reshape(blocks_dev, span * BLOCK, BLOCK),
            preferred_element_type=jnp.float32,
        )
        return spread.reshape(height, cols_dev)

    member_levels = lax.all_to_all(ensemble, "member", split_axis=1, concat_axis=0, tiled=True)

    def apply(field):
        schur = (own.astype(jnp.float32) * field).astype(jnp.bfloat16)
        lifted = jnp.dot(vertical, schur, preferred_element_type=jnp.float32).astype(jnp.bfloat16)
        swapped = lax.all_to_all(lifted[None], "member", split_axis=1, concat_axis=0, tiled=True)
        count_m, share = (swapped.shape[0], swapped.shape[1])
        spread = horizontal(swapped.reshape(count_m * share, cols_dev)).reshape(
            count_m, share, cols_dev
        )
        summed = jnp.sum(member_levels.astype(jnp.float32) * spread, axis=0) / (members - 1)
        return lax.all_gather(summed, "member", axis=0, tiled=True)

    first = apply(state)
    second = apply(first)
    return (first, second)


def solution(mesh):
    in_specs = (
        P(None, "space"),
        P("member", None, "space"),
        P(),
        P(None, "space"),
        P(None, "space"),
        P("space"),
    )
    out_specs = (P(None, "space"), P(None, "space"))
    return jax.shard_map(
        on_device, mesh=mesh, in_specs=in_specs, out_specs=out_specs, check_vma=False
    )
```

profile of v0, /device:TPU:0, one launch (start us, length us, event | category | flops | bytes accessed | tf_op | source)
XLA Modules:
  0.0 152.5 jit_solution(12569182766592238632)
XLA Ops:
  0.6 0.0 copy-start
  0.6 0.7 fusion.69
  1.4 2.9 %collective-permute-start = (s32[2,256]{1,0:T(2,128)S(1)}, s32[2,256]{1,0:T(2,128)S(1)}, u32[]{:S(2)}, u32[]{:S(2)}) collective-permute-start(s32[2,256]{1,0:T(2,128)S(1)} %get-tuple-element.20), channel_id=1, source_target_pairs={{0,4},{4,8},{8,12},{12,16},{16,20},{20,24},{24,28},{28,0},{1,5},{5... | collective-permute-start | bytes 6152 | tf_op jit(solution)/shard_map/ppermute | solution.py:19
  4.3 3.0 %collective-permute-start.1 = (s32[2,256]{1,0:T(2,128)S(1)}, s32[2,256]{1,0:T(2,128)S(1)}, u32[]{:S(2)}, u32[]{:S(2)}) collective-permute-start(s32[2,256]{1,0:T(2,128)S(1)} %get-tuple-element.21), channel_id=1, source_target_pairs={{4,0},{8,4},{12,8},{16,12},{20,16},{24,20},{28,24},{0,28},{5,1},{9... | collective-permute-start | bytes 6152 | tf_op jit(solution)/shard_map/ppermute | solution.py:22
  7.3 1.5 fusion.12
  8.8 0.0 copy-start.2
  8.8 0.0 copy-start.3
  8.8 0.0 copy-start.1
  8.9 0.6 copy.112
  9.5 0.5 broadcast.198
  10.0 3.0 %reduce = bf16[32,6144]{1,0:T(8,128)(2,1)S(1)} reduce(bf16[32,1,6144]{2,1,0:T(2,128)(2,1)S(1)} %bitcast.66, bf16[]{:T(256)} %broadcast.198), dimensions={1}, to_apply=%bitcast.60.reduce_sub_computation | reduce | bytes 786434
  13.1 1.2 reshape.94
  14.2 3.5 %all-to-all-start.1 = ((bf16[4,2,24576]{2,1,0:T(2,128)(2,1)}), bf16[4,2,24576]{2,1,0:T(2,128)(2,1)S(1)}, u32[]{:S(2)}, u32[]{:S(2)}) async-start(bf16[4,2,24576]{2,1,0:T(2,128)(2,1)} %reshape.94), calls=%async_computation.1 | async-start | bytes 786432 | tf_op jit(solution)/shard_map/all_to_all | solution.py:93
  18.4 0.1 fusion.33
  18.6 0.6 copy.113
  19.2 0.1 reshape.92
  19.3 0.1 mul.118
  19.5 3.0 %reduce.1 = bf16[32,6144]{1,0:T(8,128)(2,1)S(1)} reduce(bf16[32,1,6144]{2,1,0:T(2,128)(2,1)S(1)} %bitcast.65, bf16[]{:T(256)} %broadcast.198), dimensions={1}, to_apply=%bitcast.61.reduce_sub_computation | reduce | bytes 786434
  22.5 1.2 reshape.96
  23.7 0.0 collective-permute-done
  23.8 1.3 all-to-all-done.1
  25.1 3.5 %all-to-all-start = ((bf16[4,2,24576]{2,1,0:T(2,128)(2,1)}), bf16[4,2,24576]{2,1,0:T(2,128)(2,1)S(1)}, u32[]{:S(2)}, u32[]{:S(2)}) async-start(bf16[4,2,24576]{2,1,0:T(2,128)(2,1)} %reshape.96), calls=%async_computation | async-start | bytes 786432 | tf_op jit(solution)/shard_map/all_to_all | solution.py:88
  28.6 0.4 reshape.95
  29.0 0.2 copy.109
  29.2 0.1 collective-permute-start.2
  29.3 4.7 %collective-permute-start.3 = (bf16[32,256]{1,0:T(8,128)(2,1)S(1)}, bf16[32,256]{1,0:T(8,128)(2,1)S(1)}, u32[]{:S(2)}, u32[]{:S(2)}) collective-permute-start(bf16[32,256]{1,0:T(8,128)(2,1)S(1)} %get-tuple-element.15), channel_id=1, source_target_pairs={{4,0},{8,4},{12,8},{16,12},{20,16},{24,20},{28,24},{0,28},{5,1},{9... | collective-permute-start | bytes 49160 | tf_op jit(solution)/shard_map/ppermute | solution.py:22
  34.0 1.9 %all-to-all-done = bf16[4,2,24576]{2,1,0:T(2,128)(2,1)S(1)} async-done(((bf16[4,2,24576]{2,1,0:T(2,128)(2,1)}), bf16[4,2,24576]{2,1,0:T(2,128)(2,1)S(1)}, u32[]{:S(2)}, u32[]{:S(2)}) %all-to-all-start) | async-done | bytes 393248 | tf_op jit(solution)/shard_map/all_to_all | solution.py:88
  36.0 0.4 reshape.97
  36.4 0.2 reshape.88
  36.7 0.3 fusion.65
  37.0 0.1 copy_dynamic-update-slice_fusion.9
  37.1 0.2 copy_dynamic-update-slice_fusion.8
  37.3 0.2 copy_dynamic-update-slice_fusion.7
  37.5 0.2 copy_dynamic-update-slice_fusion.6
  37.7 0.2 copy_dynamic-update-slice_fusion.5
  37.9 36.2 %fusion.21 = f32[32,48,128]{2,0,1:T(8,128)S(1)} fusion(bf16[32,48,640]{2,0,1:T(8,128)(2,1)S(1)} %copy_dynamic-update-slice_fusion.5, s32[48,128]{1,0:T(8,128)S(1)} %bitcast.79, s32[48,640]{1,0:T(8,128)S(1)} %get-tuple-element.17, s32[48,128]{1,0:T(8,128)S(1)} %bitcast.77, s32[48,640]{1,0:T(8,128)S(1)} %get-tuple-element.16, bf16[48,640]{1,0:T(8,128)(2,1)S(1)} %bitcast.75), kind=kOutput, calls=%fused_computation.26 | convolution fusion | flops 416808960 | bytes 3108864 | tf_op jit(solution)/shard_map/hno,nos->hns/dot_general | solution.py:80
  74.1 0.5 copy.69
  74.6 0.1 reshape_reshape.6
  74.7 0.3 fusion.24
  75.0 8.4 %all_gather.6 = f32[32,6144]{1,0:T(8,128)S(1)} all-gather(f32[8,6144]{1,0:T(8,128)S(1)} %broadcast_multiply_fusion.1), channel_id=1, replica_groups=mesh['space'=8,'member'=4] {'member'}, dimensions={0}, use_global_device_ids=true | all-gather | bytes 983040 | tf_op jit(solution)/shard_map/all_gather | solution.py:99
  83.4 0.2 fusion.13
  83.6 0.6 copy.111
  84.3 3.0 %reduce.2 = bf16[32,6144]{1,0:T(8,128)(2,1)S(1)} reduce(bf16[32,1,6144]{2,1,0:T(2,128)(2,1)S(1)} %bitcast.67, bf16[]{:T(256)} %broadcast.198), dimensions={1}, to_apply=%bitcast.59.reduce_sub_computation | reduce | bytes 786434
  87.3 0.4 reshape.98
  87.7 9.8 %all_to_all.12 = bf16[4,2,24576]{2,1,0:T(2,128)(2,1)S(1)} all-to-all(bf16[4,2,24576]{2,1,0:T(2,128)(2,1)S(1)} %reshape.98), channel_id=1, replica_groups=mesh['space'=8,'member'=4] {'member'}, dimensions={0} | all-to-all | bytes 786432 | tf_op jit(solution)/shard_map/all_to_all | solution.py:93
  97.6 0.4 reshape.99
  98.0 0.2 copy.108
  98.2 0.1 collective-permute-start.4
  98.3 4.8 %collective-permute-start.5 = (bf16[32,256]{1,0:T(8,128)(2,1)S(1)}, bf16[32,256]{1,0:T(8,128)(2,1)S(1)}, u32[]{:S(2)}, u32[]{:S(2)}) collective-permute-start(bf16[32,256]{1,0:T(8,128)(2,1)S(1)} %get-tuple-element.13), channel_id=1, source_target_pairs={{4,0},{8,4},{12,8},{16,12},{20,16},{24,20},{28,24},{0,28},{5,1},{9... | collective-permute-start | bytes 49160 | tf_op jit(solution)/shard_map/ppermute | solution.py:22
  103.1 1.7 %collective-permute-done.4 = bf16[32,256]{1,0:T(8,128)(2,1)S(1)} collective-permute-done((bf16[32,256]{1,0:T(8,128)(2,1)S(1)}, bf16[32,256]{1,0:T(8,128)(2,1)S(1)}, u32[]{:S(2)}, u32[]{:S(2)}) %collective-permute-start.4) | collective-permute-done | bytes 16416 | tf_op jit(solution)/shard_map/ppermute | solution.py:19
  104.7 0.2 reshape.90
  105.0 0.3 fusion.64
  105.3 0.1 copy_dynamic-update-slice_fusion.4
  105.5 0.2 copy_dynamic-update-slice_fusion.3
  105.6 0.2 copy_dynamic-update-slice_fusion.2
  105.8 0.2 copy_dynamic-update-slice_fusion.1
  106.0 0.2 copy_dynamic-update-slice_fusion
  106.2 36.2 %fusion.18 = f32[32,48,128]{2,0,1:T(8,128)S(1)} fusion(bf16[32,48,640]{2,0,1:T(8,128)(2,1)S(1)} %copy_dynamic-update-slice_fusion, s32[48,128]{1,0:T(8,128)S(1)} %bitcast.80, s32[48,640]{1,0:T(8,128)S(1)} %get-tuple-element.17, s32[48,128]{1,0:T(8,128)S(1)} %bitcast.78, s32[48,640]{1,0:T(8,128)S(1)} %get-tuple-element.16, bf16[48,640]{1,0:T(8,128)(2,1)S(1)} %bitcast.76), kind=kOutput, calls=%fused_computation.25 | convolution fusion | flops 416808960 | bytes 3108864 | tf_op jit(solution)/shard_map/hno,nos->hns/dot_general | solution.py:80
  142.4 0.5 copy.76
  142.9 0.1 reshape_reshape.7
  143.0 0.3 fusion.25
  143.3 7.5 %all_gather.7 = f32[32,6144]{1,0:T(8,128)S(1)} all-gather(f32[8,6144]{1,0:T(8,128)S(1)} %broadcast_multiply_fusion), channel_id=1, replica_groups=mesh['space'=8,'member'=4] {'member'}, dimensions={0}, use_global_device_ids=true | all-gather | bytes 983040 | tf_op jit(solution)/shard_map/all_gather | solution.py:99
  150.8 0.9 copy.129
  151.6 0.9 copy.130
  (27 shorter events, 0.3 us)
Async XLA Ops:
  0.6 6.7 %copy-start = (bf16[32,32]{1,0:T(8,128)(2,1)S(1)}, bf16[32,32]{1,0:T(8,128)(2,1)}, u32[]{:S(2)}) copy-start(bf16[32,32]{1,0:T(8,128)(2,1)} %param.8) | copy-start | bytes 6148
  1.4 22.3 %collective-permute-start = (s32[2,256]{1,0:T(2,128)S(1)}, s32[2,256]{1,0:T(2,128)S(1)}, u32[]{:S(2)}, u32[]{:S(2)}) collective-permute-start(s32[2,256]{1,0:T(2,128)S(1)} %get-tuple-element.20), channel_id=1, source_target_pairs={{0,4},{4,8},{8,12},{12,16},{16,20},{20,24},{24,28},{28,0},{1,5},{5... | collective-permute-start | bytes 6152 | tf_op jit(solution)/shard_map/ppermute | solution.py:19
  4.3 19.4 %collective-permute-start.1 = (s32[2,256]{1,0:T(2,128)S(1)}, s32[2,256]{1,0:T(2,128)S(1)}, u32[]{:S(2)}, u32[]{:S(2)}) collective-permute-start(s32[2,256]{1,0:T(2,128)S(1)} %get-tuple-element.21), channel_id=1, source_target_pairs={{4,0},{8,4},{12,8},{16,12},{20,16},{24,20},{28,24},{0,28},{5,1},{9... | collective-permute-start | bytes 6152 | tf_op jit(solution)/shard_map/ppermute | solution.py:22
  8.8 8.9 %copy-start.2 = (s32[2,6144]{1,0:T(2,128)S(1)}, s32[2,6144]{1,0:T(2,128)}, u32[]{:S(2)}) copy-start(s32[2,6144]{1,0:T(2,128)} %param.9) | copy-start | bytes 147460
  8.8 9.6 %copy-start.3 = (s32[2,240]{1,0:T(2,128)S(1)}, s32[2,240]{1,0:T(2,128)}, u32[]{:S(2)}) copy-start(s32[2,240]{1,0:T(2,128)} %param.10) | copy-start | bytes 5764
  8.8 9.7 %copy-start.1 = (bf16[1,32,6144]{2,1,0:T(8,128)(2,1)S(1)}, bf16[1,32,6144]{2,1,0:T(8,128)(2,1)}, u32[]{:S(2)}) copy-start(bf16[1,32,6144]{2,1,0:T(8,128)(2,1)} %param.7) | copy-start | bytes 1179652
  14.2 10.9 %all-to-all-start.1 = ((bf16[4,2,24576]{2,1,0:T(2,128)(2,1)}), bf16[4,2,24576]{2,1,0:T(2,128)(2,1)S(1)}, u32[]{:S(2)}, u32[]{:S(2)}) async-start(bf16[4,2,24576]{2,1,0:T(2,128)(2,1)} %reshape.94), calls=%async_computation.1 | async-start | bytes 786432 | tf_op jit(solution)/shard_map/all_to_all | solution.py:93
  25.1 10.9 %all-to-all-start = ((bf16[4,2,24576]{2,1,0:T(2,128)(2,1)}), bf16[4,2,24576]{2,1,0:T(2,128)(2,1)S(1)}, u32[]{:S(2)}, u32[]{:S(2)}) async-start(bf16[4,2,24576]{2,1,0:T(2,128)(2,1)} %reshape.96), calls=%async_computation | async-start | bytes 786432 | tf_op jit(solution)/shard_map/all_to_all | solution.py:88
  29.2 7.1 %collective-permute-start.2 = (bf16[32,256]{1,0:T(8,128)(2,1)S(1)}, bf16[32,256]{1,0:T(8,128)(2,1)S(1)}, u32[]{:S(2)}, u32[]{:S(2)}) collective-permute-start(bf16[32,256]{1,0:T(8,128)(2,1)S(1)} %get-tuple-element.14), channel_id=1, source_target_pairs={{0,4},{4,8},{8,12},{12,16},{16,20},{20,24},{24,28},{28,0},{1,5},{5... | collective-permute-start | bytes 49160 | tf_op jit(solution)/shard_map/ppermute | solution.py:19
  29.3 7.1 %collective-permute-start.3 = (bf16[32,256]{1,0:T(8,128)(2,1)S(1)}, bf16[32,256]{1,0:T(8,128)(2,1)S(1)}, u32[]{:S(2)}, u32[]{:S(2)}) collective-permute-start(bf16[32,256]{1,0:T(8,128)(2,1)S(1)} %get-tuple-element.15), channel_id=1, source_target_pairs={{4,0},{8,4},{12,8},{16,12},{20,16},{24,20},{28,24},{0,28},{5,1},{9... | collective-permute-start | bytes 49160 | tf_op jit(solution)/shard_map/ppermute | solution.py:22
  98.2 6.5 %collective-permute-start.4 = (bf16[32,256]{1,0:T(8,128)(2,1)S(1)}, bf16[32,256]{1,0:T(8,128)(2,1)S(1)}, u32[]{:S(2)}, u32[]{:S(2)}) collective-permute-start(bf16[32,256]{1,0:T(8,128)(2,1)S(1)} %get-tuple-element.12), channel_id=1, source_target_pairs={{0,4},{4,8},{8,12},{12,16},{16,20},{20,24},{24,28},{28,0},{1,5},{5... | collective-permute-start | bytes 49160 | tf_op jit(solution)/shard_map/ppermute | solution.py:19
  98.3 6.4 %collective-permute-start.5 = (bf16[32,256]{1,0:T(8,128)(2,1)S(1)}, bf16[32,256]{1,0:T(8,128)(2,1)S(1)}, u32[]{:S(2)}, u32[]{:S(2)}) collective-permute-start(bf16[32,256]{1,0:T(8,128)(2,1)S(1)} %get-tuple-element.13), channel_id=1, source_target_pairs={{4,0},{8,4},{12,8},{16,12},{20,16},{24,20},{28,24},{0,28},{5,1},{9... | collective-permute-start | bytes 49160 | tf_op jit(solution)/shard_map/ppermute | solution.py:22
where the time goes:
time: 153 us
  matrix products  74.2 us (48%)
  blocking collectives  25.7 us (17%)
  starting transfers between devices  22.5 us (15%)
  local copies, waits for them, and re-layouts  13.6 us (9%)
  other arithmetic  9.91 us (6%)
  waiting for transfers between devices  4.85 us (3%)
  between operations  1.79 us (1%)
    dot_general x2, matrix products, horizontal(): jnp.einsum('hno,nos->hns', windows, dense.reshape(blocks_dev, span * BLOC...  72.5 us
    all_gather x2, blocking collectives, apply(): return lax.all_gather(summed, 'member', axis=0, tiled=True)  15.9 us
    ppermute x3, starting transfers between devices, extended(): lax.ppermute(lax.slice_in_dim(block, 0, width, axis=dim), axis, backward)  12.5 us
    all_to_all x1, blocking collectives, apply(): lax.all_to_all(lifted[None], 'member', split_axis=1, concat_axis=0, tiled...  9.84 us
    unnamed x3, other arithmetic  9.11 us
    unnamed x33, local copies, waits for them, and re-layouts  8.64 us
    all_to_all x1, starting transfers between devices, on_device(): lax.all_to_all(ensemble, 'member', split_axis=1, concat_axis=0, tiled=True)  3.46 us
    all_to_all x1, starting transfers between devices, apply(): lax.all_to_all(lifted[None], 'member', split_axis=1, concat_axis=0, tiled...  3.46 us
  transfers between devices with their start and end apart: 8, of which 3 were waited for; matrix products, arithmetic and copies ran while one was open for 9% of the time, Pallas kernels for 0%

commit v1 on v0

v1 whole, which is shorter than its diff:
```python
import functools

import jax
import jax.numpy as jnp
from jax import lax
from jax.experimental import pallas as pl
from jax.experimental.pallas import tpu as pltpu
from jax.sharding import PartitionSpec as P

BLOCK = 128
REACH = 2
SCALE = 4.0
HALO = REACH * BLOCK
FAR = 131072.0
MESH = pl.DeviceIdType.MESH


def gaspari(r):
    near = (((-0.25 * r + 0.5) * r + 0.625) * r - 5.0 / 3.0) * r * r + 1.0
    rf = jnp.maximum(r, 1.0)
    far = (
        ((((rf / 12.0 - 0.5) * rf + 0.625) * rf + 5.0 / 3.0) * rf - 5.0) * rf
        + 4.0
        - 2.0 / (3.0 * rf)
    )
    return jnp.where(r <= 1.0, near, jnp.where(r < 2.0, far, jnp.zeros_like(r)))


def iota(shape, dim):
    return lax.broadcasted_iota(jnp.int32, shape, dim)


def dot(a, b):
    return jnp.dot(a, b, preferred_element_type=jnp.float32)


def kernel(
    tiles, members, blocks_dev, group,
    state, ens, vertical, coords, pairs, count,
    out1, out2,
    ensx, field, xy, feat, weights, lifted, own1, halo1, pack1, pack2,
    local_sem, core_recv, left_recv, right_recv, core_send, left_send, right_send,
    edge_recv, edge_send, halo_recv, halo_send, one_recv, one_send, two_recv, two_send,
):
    t = lax.axis_index("space")
    m = lax.axis_index("member")
    up = lax.rem(t + 1, tiles)
    down = lax.rem(t + tiles - 1, tiles)
    last = members - 1
    nb = blocks_dev // members
    ext = nb + 2 * REACH
    width = ext * BLOCK
    core = nb * BLOCK
    cols_dev = blocks_dev * BLOCK
    levels = state.shape[0]
    groups = nb // group
    period = cols_dev * tiles // 8
    step = BLOCK // 8
    gw = group * BLOCK
    kw = (group + 2 * REACH) * BLOCK

    def cols(start, size):
        return pl.ds(pl.multiple_of(start, BLOCK), size)

    core_x = pl.ds(HALO, core)
    left_x = pl.ds(0, HALO)
    right_x = pl.ds(HALO + core, HALO)

    barrier = pltpu.get_barrier_semaphore()
    for p in range(members):
        @pl.when(p != m)
        def _(p=p):
            pl.semaphore_signal(barrier, inc=1, device_id=(t, p), device_id_type=MESH)

        @pl.when(m == 0)
        def _(p=p):
            pl.semaphore_signal(barrier, inc=1, device_id=(down, p), device_id_type=MESH)

        @pl.when(m == last)
        def _(p=p):
            pl.semaphore_signal(barrier, inc=1, device_id=(up, p), device_id_type=MESH)

    mine = m * core
    stay = [
        pltpu.make_async_copy(
            state.at[:, cols(mine, core)], field.at[:, core_x], local_sem.at[0]),
        pltpu.make_async_copy(
            coords.at[:, cols(mine, core)], xy.at[:, core_x], local_sem.at[1]),
        pltpu.make_async_copy(
            ens.at[0, :, cols(mine, core)], ensx.at[m, :, core_x], core_recv.at[m]),
    ]
    for copy in stay:
        copy.start()

    @pl.when(m > 0)
    def _():
        at = cols(mine - HALO, HALO)
        pltpu.make_async_copy(state.at[:, at], field.at[:, left_x], edge_recv.at[0]).start()
        pltpu.make_async_copy(coords.at[:, at], xy.at[:, left_x], edge_recv.at[1]).start()
        pltpu.make_async_copy(ens.at[0, :, at], ensx.at[m, :, left_x], left_recv.at[m]).start()

    @pl.when(m < last)
    def _():
        at = cols(mine + core, HALO)
        pltpu.make_async_copy(state.at[:, at], field.at[:, right_x], edge_recv.at[2]).start()
        pltpu.make_async_copy(coords.at[:, at], xy.at[:, right_x], edge_recv.at[3]).start()
        pltpu.make_async_copy(ens.at[0, :, at], ensx.at[m, :, right_x], right_recv.at[m]).start()

    pl.semaphore_wait(barrier, members + 1)

    def remote(src, dst, send, recv, where):
        return pltpu.make_async_remote_copy(
            src_ref=src, dst_ref=dst, send_sem=send, recv_sem=recv,
            device_id=where, device_id_type=MESH)

    high = pl.ds(cols_dev - HALO, HALO)
    low = pl.ds(0, HALO)
    edge_up = [
        remote(coords.at[:, high], xy.at[:, left_x], edge_send.at[1], edge_recv.at[1], (up, 0)),
        remote(state.at[:, high], field.at[:, left_x], edge_send.at[0], edge_recv.at[0], (up, 0)),
    ]
    edge_down = [
        remote(coords.at[:, low], xy.at[:, right_x], edge_send.at[3], edge_recv.at[3], (down, last)),
        remote(state.at[:, low], field.at[:, right_x], edge_send.at[2], edge_recv.at[2], (down, last)),
    ]

    @pl.when(m == last)
    def _():
        for copy in edge_up:
            copy.start()

    @pl.when(m == 0)
    def _():
        for copy in edge_down:
            copy.start()

    def core_copy(p):
        return remote(
            ens.at[0, :, pl.ds(p * core, core)], ensx.at[m, :, core_x],
            core_send.at[p], core_recv.at[m], (t, p))

    def left_copy(p):
        if p == 0:
            return remote(
                ens.at[0, :, high], ensx.at[m, :, left_x],
                left_send.at[p], left_recv.at[m], (up, 0))
        return remote(
            ens.at[0, :, pl.ds(p * core - HALO, HALO)], ensx.at[m, :, left_x],
            left_send.at[p], left_recv.at[m], (t, p))

    def right_copy(p):
        if p == last:
            return remote(
                ens.at[0, :, low], ensx.at[m, :, right_x],
                right_send.at[p], right_recv.at[m], (down, last))
        return remote(
            ens.at[0, :, pl.ds((p + 1) * core, HALO)], ensx.at[m, :, right_x],
            right_send.at[p], right_recv.at[m], (t, p))

    left_copy(0).start()
    right_copy(last).start()
    for p in range(members):
        @pl.when(p != m)
        def _(p=p):
            core_copy(p).start()
            if p != 0:
                left_copy(p).start()
            if p != last:
                right_copy(p).start()

    def arrived(ref, sem):
        pltpu.make_async_copy(ref, ref, sem).wait()

    stay[1].wait()
    arrived(xy.at[:, left_x], edge_recv.at[1])
    arrived(xy.at[:, right_x], edge_recv.at[3])
    lane = iota((1, width), 1)
    block = lane >> 7
    rel = xy[0:1, :] - step * (t * blocks_dev + m * nb - REACH + block)
    rel = jnp.where(rel < 0, rel + period, rel)
    rel = jnp.where(rel >= period, rel - period, rel)
    along = rel + step * block - (step * ext // 2 + 31)
    across = xy[1:2, :]
    square = along * along + across * across
    upper = ((square >> 7) << 7).astype(jnp.float32)
    lower = (square & 127).astype(jnp.float32)
    along = along.astype(jnp.float32)
    across = across.astype(jnp.float32)

    def rows(parts, size):
        row = iota((16, size), 0)
        table = jnp.zeros((16, size), jnp.float32)
        for i, part in enumerate(parts):
            table = jnp.where(row == i, part, table)
        return table

    blocks_x = (iota((16, width), 0) == (iota((16, width), 1) >> 7)).astype(jnp.float32)
    source = jnp.concatenate(
        [rows([along, across, upper, lower, 1.0, 1.0], width), blocks_x], axis=0)
    feat[...] = jnp.transpose(source).astype(jnp.bfloat16)

    slots = pairs.shape[1]
    first_block = m * nb + iota((16, slots), 0)
    live = iota((16, slots), 1) < count[0]
    is_dst = ((pairs[0:1, :] == first_block) & live).astype(jnp.float32).astype(jnp.bfloat16)
    is_src = (pairs[1:2, :] == first_block).astype(jnp.float32).astype(jnp.bfloat16)
    present = lax.dot_general(
        is_src, is_dst, (((1,), (1,)), ((), ())), preferred_element_type=jnp.float32)
    spread_out = (iota((16, core), 0) == (iota((16, core), 1) >> 7)).astype(jnp.float32)
    present = dot(present.astype(jnp.bfloat16), spread_out.astype(jnp.bfloat16))
    absent = jnp.where(present > 0.5, 0.0, FAR)
    own = slice(HALO, HALO + core)
    target = jnp.concatenate(
        [rows([-2.0 * along[:, own], -2.0 * across[:, own], 1.0, 1.0,
               upper[:, own], lower[:, own]], core), absent], axis=0).astype(jnp.bfloat16)

    dist = jnp.sqrt(iota((8, BLOCK), 1).astype(jnp.float32))
    table = gaspari(dist / SCALE).astype(jnp.bfloat16).astype(jnp.float32)
    table = jnp.broadcast_to(table[0:1, :], (BLOCK, BLOCK))
    for g in range(groups):
        for s in range(group + 2 * REACH):
            at = (g * group + s) * BLOCK
            d2 = dot(feat[at:at + BLOCK, :], target[:, g * gw:(g + 1) * gw])
            index = jnp.minimum(d2, 127.0).astype(jnp.int32)
            for j in range(group):
                w = jnp.take_along_axis(
                    table, index[:, j * BLOCK:(j + 1) * BLOCK], axis=1,
                    mode="promise_in_bounds")
                weights[g, s * BLOCK:(s + 1) * BLOCK, j * BLOCK:(j + 1) * BLOCK] = w.astype(
                    jnp.bfloat16)

    batch = 4 if members % 4 == 0 else 1
    tall = batch * levels
    pick = (iota((tall, levels), 0) % levels == iota((tall, levels), 1)).astype(
        jnp.float32).astype(jnp.bfloat16)
    turn = (iota((levels, tall), 1) % levels == iota((levels, tall), 0)).astype(
        jnp.float32).astype(jnp.bfloat16)
    stacked = dot(dot(pick, vertical[...]).astype(jnp.bfloat16), turn)
    same = iota((tall, tall), 0) // levels == iota((tall, tall), 1) // levels
    diagonal = jnp.where(same, stacked, 0.0).astype(jnp.bfloat16)

    def lift(at, size, values):
        for b in range(members // batch):
            schur = [
                (ensx[b * batch + i, :, at:at + size].astype(jnp.float32) * values).astype(
                    jnp.bfloat16)
                for i in range(batch)
            ]
            product = dot(diagonal, jnp.concatenate(schur, axis=0))
            lifted[b * tall:(b + 1) * tall, at:at + size] = product.astype(jnp.bfloat16)

    def summed(g):
        spread = dot(lifted[:, g * gw:g * gw + kw], weights[g])
        at = HALO + g * gw
        total = jnp.zeros((levels, gw), jnp.float32)
        for i in range(members):
            total += ensx[i, :, at:at + gw].astype(jnp.float32) * spread[
                i * levels:(i + 1) * levels, :]
        return total / (members - 1)

    edges = REACH // group if REACH % group == 0 else groups
    order = list(dict.fromkeys(
        list(range(min(edges, groups)))
        + list(range(max(groups - edges, 0), groups))
        + list(range(groups))))
    inner_first = order[::-1]

    stay[0].wait()
    arrived(field.at[:, left_x], edge_recv.at[0])
    arrived(field.at[:, right_x], edge_recv.at[2])
    for i in range(members):
        arrived(ensx.at[i, :, core_x], core_recv.at[i])
        arrived(ensx.at[i, :, left_x], left_recv.at[i])
        arrived(ensx.at[i, :, right_x], right_recv.at[i])
    for e in range(0, ext, 2) if ext % 2 == 0 else range(ext):
        size = 2 * BLOCK if ext % 2 == 0 else BLOCK
        lift(e * BLOCK, size, field[:, e * BLOCK:e * BLOCK + size])

    to_left = (jnp.where(m == 0, down, t), jnp.where(m == 0, last, m - 1))
    to_right = (jnp.where(m == last, up, t), jnp.where(m == last, 0, m + 1))
    halo_copies = [
        remote(own1.at[:, pl.ds(0, HALO)], halo1.at[1], halo_send.at[0], halo_recv.at[1], to_left),
        remote(own1.at[:, pl.ds(core - HALO, HALO)], halo1.at[0],
               halo_send.at[1], halo_recv.at[0], to_right),
    ]
    sent = [False, False]
    done = set()
    for g in order:
        result = summed(g)
        own1[:, g * gw:(g + 1) * gw] = result
        pack1[:, g * gw:(g + 1) * gw] = result.astype(jnp.bfloat16)
        done.add(g)
        for side, need in enumerate((
            {k for k in range(groups) if k * gw < HALO},
            {k for k in range(groups) if (k + 1) * gw > core - HALO},
        )):
            if not sent[side] and need <= done:
                halo_copies[side].start()
                sent[side] = True

    own_cols = cols(mine, core)

    def one_copy(p):
        return remote(pack1, out1.at[:, own_cols], one_send.at[p], one_recv.at[m], (t, p))

    def two_copy(p, g):
        return remote(
            pack2.at[:, pl.ds(g * gw, gw)], out2.at[:, cols(mine + g * gw, gw)],
            two_send.at[p, g], two_recv.at[m, g], (t, p))

    for p in range(members):
        @pl.when(p != m)
        def _(p=p):
            one_copy(p).start()
    keep1 = pltpu.make_async_copy(pack1, out1.at[:, own_cols], one_recv.at[m])
    keep1.start()

    for g in range(groups):
        lift(HALO + g * gw, gw, own1[:, g * gw:(g + 1) * gw])
    halves = [False, False]
    keep2 = []
    for g in inner_first:
        if not halves[0] and g * gw < HALO:
            halo_copies[1].wait_recv()
            lift(0, HALO, halo1[0])
            halves[0] = True
        if not halves[1] and (g + 1) * gw > core - HALO:
            halo_copies[0].wait_recv()
            lift(HALO + core, HALO, halo1[1])
            halves[1] = True
        pack2[:, g * gw:(g + 1) * gw] = summed(g).astype(jnp.bfloat16)
        for p in range(members):
            @pl.when(p != m)
            def _(p=p, g=g):
                two_copy(p, g).start()
        keep = pltpu.make_async_copy(
            pack2.at[:, pl.ds(g * gw, gw)], out2.at[:, cols(mine + g * gw, gw)],
            two_recv.at[m, g])
        keep.start()

    for side in range(2):
        halo_copies[side].wait_send()

    @pl.when(m == last)
    def _():
        for copy in edge_up:
            copy.wait_send()

    @pl.when(m == 0)
    def _():
        for copy in edge_down:
            copy.wait_send()

    left_copy(0).wait_send()
    right_copy(last).wait_send()
    for p in range(members):
        @pl.when(p != m)
        def _(p=p):
            core_copy(p).wait_send()
            if p != 0:
                left_copy(p).wait_send()
            if p != last:
                right_copy(p).wait_send()
            one_copy(p).wait_send()
            for g in range(groups):
                two_copy(p, g).wait_send()
    for i in range(members):
        arrived(out1.at[:, pl.ds(i * core, core)], one_recv.at[i])
        for g in range(groups):
            arrived(out2.at[:, pl.ds(i * core + g * gw, gw)], two_recv.at[i, g])


def on_device(tiles, members, state, ensemble, vertical, coords, pairs, pair_count):
    levels, cols_dev = state.shape
    blocks_dev = cols_dev // BLOCK
    nb = blocks_dev // members
    group = 2 if nb % 2 == 0 else 1
    groups = nb // group
    core = nb * BLOCK
    width = core + 2 * HALO
    dma = pltpu.SemaphoreType.DMA
    vmem = pl.BlockSpec(memory_space=pltpu.VMEM)
    hbm = pl.BlockSpec(memory_space=pl.ANY)
    smem = pl.BlockSpec(memory_space=pltpu.SMEM)
    first, second = pl.pallas_call(
        functools.partial(kernel, tiles, members, blocks_dev, group),
        out_shape=[jax.ShapeDtypeStruct((levels, cols_dev), jnp.bfloat16)] * 2,
        in_specs=[hbm, hbm, vmem, hbm, vmem, smem],
        out_specs=[hbm, hbm],
        scratch_shapes=[
            pltpu.VMEM((members, levels, width), jnp.bfloat16),
            pltpu.VMEM((levels, width), jnp.float32),
            pltpu.VMEM((2, width), jnp.int32),
            pltpu.VMEM((width, 32), jnp.bfloat16),
            pltpu.VMEM((groups, (group + 2 * REACH) * BLOCK, group * BLOCK), jnp.bfloat16),
            pltpu.VMEM((members * levels, width), jnp.bfloat16),
            pltpu.VMEM((levels, core), jnp.float32),
            pltpu.VMEM((2, levels, HALO), jnp.float32),
            pltpu.VMEM((levels, core), jnp.bfloat16),
            pltpu.VMEM((levels, core), jnp.bfloat16),
            dma((2,)),
            dma((members,)), dma((members,)), dma((members,)),
            dma((members,)), dma((members,)), dma((members,)),
            dma((4,)), dma((4,)),
            dma((2,)), dma((2,)),
            dma((members,)), dma((members,)),
            dma((members, groups)), dma((members, groups)),
        ],
        compiler_params=pltpu.CompilerParams(
            collective_id=0, has_side_effects=True, vmem_limit_bytes=40 * 1024 * 1024
        ),
    )(state, ensemble, vertical, coords, pairs, pair_count)
    return first.astype(jnp.float32), second.astype(jnp.float32)


def solution(mesh):
    in_specs = (
        P(None, "space"),
        P("member", None, "space"),
        P(),
        P(None, "space"),
        P(None, "space"),
        P("space"),
    )
    out_specs = (P(None, "space"), P(None, "space"))
    return jax.shard_map(
        functools.partial(on_device, mesh.shape["space"], mesh.shape["member"]),
        mesh=mesh, in_specs=in_specs, out_specs=out_specs, check_vma=False,
    )
```

time: 153 us -> 32.5 us (0.21)
  matrix products: 74.2 us -> 0 us
  blocking collectives: 25.7 us -> 0 us
  Pallas kernels: 0 us -> 24.7 us
  starting transfers between devices: 22.5 us -> 0 us
  local copies, waits for them, and re-layouts: 13.6 us -> 4.3 us
  other arithmetic: 9.91 us -> 1.86 us
  waiting for transfers between devices: 4.85 us -> 0 us
    dot_general x4 -> x0, matrix products: 74.2 us -> none  [the longest x2 72.5 us: horizontal(): jnp.einsum('hno,nos->hns', windows, dense.reshape(blocks_dev, span * BLOC...]
    pallas_call x0 -> x1, Pallas kernels: none -> 24.7 us  [on_device(): pl.pallas_call(functools.partial(kernel, tiles, members, blocks_dev, grou...]
    all_gather x2 -> x0, blocking collectives: 15.9 us -> none  [apply(): return lax.all_gather(summed, 'member', axis=0, tiled=True)]
    ppermute x6 -> x0, starting transfers between devices: 15.6 us -> none  [the longest x3 12.5 us: extended(): lax.ppermute(lax.slice_in_dim(block, 0, width, axis=dim), axis, backward)]
    all_to_all x1 -> x0, blocking collectives: 9.84 us -> none  [apply(): lax.all_to_all(lifted[None], 'member', split_axis=1, concat_axis=0, tiled...]
    unnamed x3 -> x0, other arithmetic: 9.11 us -> none
    all_to_all x2 -> x0, starting transfers between devices: 6.92 us -> none  [the longest x1 3.46 us: on_device(): lax.all_to_all(ensemble, 'member', split_axis=1, concat_axis=0, tiled=True)]
    unnamed x33 -> x10, local copies, waits for them, and re-layouts: 8.64 us -> 4.3 us
  transfers between devices with their start and end apart: 8 -> 0, of which waited for: 3 -> 0; matrix products, arithmetic and copies ran while one was open for 9% -> 0% of each run, Pallas kernels for 0% -> 0%
where the time goes in v1:
time: 32.5 us; the launch traced here: 32.2 us
  Pallas kernels  24.7 us (76%)
  local copies, waits for them, and re-layouts  4.3 us (13%)
  other arithmetic  1.86 us (6%)
  between operations  1.3 us (4%)
    pallas_call x1, Pallas kernels, on_device(): pl.pallas_call(functools.partial(kernel, tiles, members, blocks_dev, grou...  24.7 us
    unnamed x10, local copies, waits for them, and re-layouts  4.3 us
    convert_element_type x2, other arithmetic, on_device(): return (first.astype(jnp.float32), second.astype(jnp.float32))  1.86 us

profile of v1, /device:TPU:0, one launch (start us, length us, event | category | flops | bytes accessed | tf_op | source)
XLA Modules:
  0.0 32.2 jit_solution(14833970533099908450)
XLA Ops:
  1.3 0.0 copy-start
  1.3 1.1 %copy-done = f32[32,6144]{1,0:T(8,128)S(1)} copy-done((f32[32,6144]{1,0:T(8,128)S(1)}, f32[32,6144]{1,0:T(8,128)}, u32[]{:S(2)}) %copy-start) | copy-done | bytes 786456
  2.4 0.0 copy-start.1
  2.4 1.0 %copy-done.1 = bf16[1,32,6144]{2,1,0:T(8,128)(2,1)S(1)} copy-done((bf16[1,32,6144]{2,1,0:T(8,128)(2,1)S(1)}, bf16[1,32,6144]{2,1,0:T(8,128)(2,1)}, u32[]{:S(2)}) %copy-start.1) | copy-done | bytes 393240
  3.4 0.0 copy-start.2
  3.4 0.8 %copy-done.2 = s32[2,6144]{1,0:T(2,128)S(1)} copy-done((s32[2,6144]{1,0:T(2,128)S(1)}, s32[2,6144]{1,0:T(2,128)}, u32[]{:S(2)}) %copy-start.2) | copy-done | bytes 49176
  4.2 0.0 copy-start.3
  4.2 0.7 %copy-done.3 = bf16[32,32]{1,0:T(8,128)(2,1)S(1)} copy-done((bf16[32,32]{1,0:T(8,128)(2,1)S(1)}, bf16[32,32]{1,0:T(8,128)(2,1)}, u32[]{:S(2)}) %copy-start.3) | copy-done | bytes 2072
  4.9 0.0 copy-start.4
  4.9 0.7 %copy-done.4 = s32[2,240]{1,0:T(2,128)S(1)} copy-done((s32[2,240]{1,0:T(2,128)S(1)}, s32[2,240]{1,0:T(2,128)}, u32[]{:S(2)}) %copy-start.4) | copy-done | bytes 1944
  5.6 24.7 %shard_map.77 = (bf16[32,6144]{1,0:T(8,128)(2,1)S(1)}, bf16[32,6144]{1,0:T(8,128)(2,1)S(1)}) custom-call(f32[32,6144]{1,0:T(8,128)S(1)} %copy-done, bf16[1,32,6144]{2,1,0:T(8,128)(2,1)S(1)} %copy-done.1, bf16[32,32]{1,0:T(8,128)(2,1)S(1)} %copy-done.3, s32[2,6144]{1,0:T(2,128)S(1)} %copy-done.2, s32[2,240]{1,0:T(2,128)S(1)} %copy-done.4, s32[1]{0:T(128)S(6)} %copy.8.count), custom_call_target="tpu_custom_call" | custom-call | tf_op jit(solution)/shard_map/pallas_call | solution.py:385
  30.3 0.9 %convert_element_type.6 = f32[32,6144]{1,0:T(8,128)} convert(bf16[32,6144]{1,0:T(8,128)(2,1)S(1)} %get-tuple-element.4) | non-fusion elementwise | flops 196608 | bytes 1179648 | tf_op jit(solution)/shard_map/convert_element_type | solution.py:413
  31.2 0.9 %convert_element_type.7 = f32[32,6144]{1,0:T(8,128)} convert(bf16[32,6144]{1,0:T(8,128)(2,1)S(1)} %get-tuple-element.5) | non-fusion elementwise | flops 196608 | bytes 1179648 | tf_op jit(solution)/shard_map/convert_element_type | solution.py:413
Async XLA Ops:
  1.3 1.1 %copy-start = (f32[32,6144]{1,0:T(8,128)S(1)}, f32[32,6144]{1,0:T(8,128)}, u32[]{:S(2)}) copy-start(f32[32,6144]{1,0:T(8,128)} %state.1) | copy-start | bytes 2359300
  2.4 1.0 %copy-start.1 = (bf16[1,32,6144]{2,1,0:T(8,128)(2,1)S(1)}, bf16[1,32,6144]{2,1,0:T(8,128)(2,1)}, u32[]{:S(2)}) copy-start(bf16[1,32,6144]{2,1,0:T(8,128)(2,1)} %ens.1) | copy-start | bytes 1179652
  3.4 0.8 %copy-start.2 = (s32[2,6144]{1,0:T(2,128)S(1)}, s32[2,6144]{1,0:T(2,128)}, u32[]{:S(2)}) copy-start(s32[2,6144]{1,0:T(2,128)} %coords.1) | copy-start | bytes 147460
  4.2 0.7 %copy-start.3 = (bf16[32,32]{1,0:T(8,128)(2,1)S(1)}, bf16[32,32]{1,0:T(8,128)(2,1)}, u32[]{:S(2)}) copy-start(bf16[32,32]{1,0:T(8,128)(2,1)} %vertical.1) | copy-start | bytes 6148
  4.9 0.7 %copy-start.4 = (s32[2,240]{1,0:T(2,128)S(1)}, s32[2,240]{1,0:T(2,128)}, u32[]{:S(2)}) copy-start(s32[2,240]{1,0:T(2,128)} %pairs.1) | copy-start | bytes 5764

commit v2 on v1

--- a/solution.py
+++ b/solution.py
@@ -36,11 +36,12 @@
 
 def kernel(
     tiles, members, blocks_dev, group,
-    state, ens, vertical, coords, pairs, count,
+    state, ens, vertical_in, coords, pairs_in, count,
     out1, out2,
-    ensx, field, xy, feat, weights, lifted, own1, halo1, pack1, pack2,
+    vertical, pairs, ensx, field, xy, feat, weights, lifted, own1, halo1, pack1, pack2,
     local_sem, core_recv, left_recv, right_recv, core_send, left_send, right_send,
     edge_recv, edge_send, halo_recv, halo_send, one_recv, one_send, two_recv, two_send,
+    one_fwd, two_fwd,
 ):
     t = lax.axis_index("space")
     m = lax.axis_index("member")
@@ -81,6 +82,10 @@
             pl.semaphore_signal(barrier, inc=1, device_id=(up, p), device_id_type=MESH)
 
     mine = m * core
+    small = [
+        pltpu.make_async_copy(pairs_in, pairs, local_sem.at[2]),
+        pltpu.make_async_copy(vertical_in, vertical, local_sem.at[3]),
+    ]
     stay = [
         pltpu.make_async_copy(
             state.at[:, cols(mine, core)], field.at[:, core_x], local_sem.at[0]),
@@ -89,8 +94,11 @@
         pltpu.make_async_copy(
             ens.at[0, :, cols(mine, core)], ensx.at[m, :, core_x], core_recv.at[m]),
     ]
-    for copy in stay:
+    stay[1].start()
+    for copy in small:
         copy.start()
+    stay[0].start()
+    stay[2].start()
 
     @pl.when(m > 0)
     def _():
@@ -106,6 +114,9 @@
         pltpu.make_async_copy(coords.at[:, at], xy.at[:, right_x], edge_recv.at[3]).start()
         pltpu.make_async_copy(ens.at[0, :, at], ensx.at[m, :, right_x], right_recv.at[m]).start()
 
+    dist = jnp.sqrt(iota((8, BLOCK), 1).astype(jnp.float32))
+    table = gaspari(dist / SCALE).astype(jnp.bfloat16).astype(jnp.float32)
+    table = jnp.broadcast_to(table[0:1, :], (BLOCK, BLOCK))
     pl.semaphore_wait(barrier, members + 1)
 
     def remote(src, dst, send, recv, where):
@@ -170,6 +181,28 @@
 
     def arrived(ref, sem):
         pltpu.make_async_copy(ref, ref, sem).wait()
+
+    small[0].wait()
+    slots = pairs.shape[1]
+    first_block = m * nb + iota((16, slots), 0)
+    live = iota((16, slots), 1) < count[0]
+    is_dst = ((pairs[0:1, :] == first_block) & live).astype(jnp.float32).astype(jnp.bfloat16)
+    is_src = (pairs[1:2, :] == first_block).astype(jnp.float32).astype(jnp.bfloat16)
+    present = lax.dot_general(
+        is_src, is_dst, (((1,), (1,)), ((), ())), preferred_element_type=jnp.float32)
+    spread_out = (iota((16, core), 0) == (iota((16, core), 1) >> 7)).astype(jnp.float32)
+    present = dot(present.astype(jnp.bfloat16), spread_out.astype(jnp.bfloat16))
+    absent = jnp.where(present > 0.5, 0.0, FAR)
+    small[1].wait()
+    batch = 4 if members % 4 == 0 else 1
+    tall = batch * levels
+    pick = (iota((tall, levels), 0) % levels == iota((tall, levels), 1)).astype(
+        jnp.float32).astype(jnp.bfloat16)
+    turn = (iota((levels, tall), 1) % levels == iota((levels, tall), 0)).astype(
+        jnp.float32).astype(jnp.bfloat16)
+    stacked = dot(dot(pick, vertical[...]).astype(jnp.bfloat16), turn)
+    same = iota((tall, tall), 0) // levels == iota((tall, tall), 1) // levels
+    diagonal = jnp.where(same, stacked, 0.0).astype(jnp.bfloat16)
 
     stay[1].wait()
     arrived(xy.at[:, left_x], edge_recv.at[1])
@@ -199,24 +232,11 @@
         [rows([along, across, upper, lower, 1.0, 1.0], width), blocks_x], axis=0)
     feat[...] = jnp.transpose(source).astype(jnp.bfloat16)
 
-    slots = pairs.shape[1]
-    first_block = m * nb + iota((16, slots), 0)
-    live = iota((16, slots), 1) < count[0]
-    is_dst = ((pairs[0:1, :] == first_block) & live).astype(jnp.float32).astype(jnp.bfloat16)
-    is_src = (pairs[1:2, :] == first_block).astype(jnp.float32).astype(jnp.bfloat16)
-    present = lax.dot_general(
-        is_src, is_dst, (((1,), (1,)), ((), ())), preferred_element_type=jnp.float32)
-    spread_out = (iota((16, core), 0) == (iota((16, core), 1) >> 7)).astype(jnp.float32)
-    present = dot(present.astype(jnp.bfloat16), spread_out.astype(jnp.bfloat16))
-    absent = jnp.where(present > 0.5, 0.0, FAR)
     own = slice(HALO, HALO + core)
     target = jnp.concatenate(
         [rows([-2.0 * along[:, own], -2.0 * across[:, own], 1.0, 1.0,
                upper[:, own], lower[:, own]], core), absent], axis=0).astype(jnp.bfloat16)
 
-    dist = jnp.sqrt(iota((8, BLOCK), 1).astype(jnp.float32))
-    table = gaspari(dist / SCALE).astype(jnp.bfloat16).astype(jnp.float32)
-    table = jnp.broadcast_to(table[0:1, :], (BLOCK, BLOCK))
     for g in range(groups):
         for s in range(group + 2 * REACH):
             at = (g * group + s) * BLOCK
@@ -228,16 +248,6 @@
                     mode="promise_in_bounds")
                 weights[g, s * BLOCK:(s + 1) * BLOCK, j * BLOCK:(j + 1) * BLOCK] = w.astype(
                     jnp.bfloat16)
-
-    batch = 4 if members % 4 == 0 else 1
-    tall = batch * levels
-    pick = (iota((tall, levels), 0) % levels == iota((tall, levels), 1)).astype(
-        jnp.float32).astype(jnp.bfloat16)
-    turn = (iota((levels, tall), 1) % levels == iota((levels, tall), 0)).astype(
-        jnp.float32).astype(jnp.bfloat16)
-    stacked = dot(dot(pick, vertical[...]).astype(jnp.bfloat16), turn)
-    same = iota((tall, tall), 0) // levels == iota((tall, tall), 1) // levels
-    diagonal = jnp.where(same, stacked, 0.0).astype(jnp.bfloat16)
 
     def lift(at, size, values):
         for b in range(members // batch):
@@ -308,10 +318,25 @@
             pack2.at[:, pl.ds(g * gw, gw)], out2.at[:, cols(mine + g * gw, gw)],
             two_send.at[p, g], two_recv.at[m, g], (t, p))
 
+    sibling = m + 1 - 2 * lax.rem(m, 2)
+
+    def abroad(p):
+        return (p != m) & (lax.rem(m, 2) == p % 2)
+
+    def one_pass(p):
+        at = pl.ds(p * core, core)
+        return remote(out1.at[:, at], out1.at[:, at], one_fwd.at[p], one_recv.at[p], (t, sibling))
+
+    def two_pass(p, g):
+        at = pl.ds(p * core + g * gw, gw)
+        return remote(
+            out2.at[:, at], out2.at[:, at], two_fwd.at[p, g], two_recv.at[p, g], (t, sibling))
+
     for p in range(members):
-        @pl.when(p != m)
+        @pl.when(abroad(p))
         def _(p=p):
             one_copy(p).start()
+    one_copy(sibling).start()
     keep1 = pltpu.make_async_copy(pack1, out1.at[:, own_cols], one_recv.at[m])
     keep1.start()
 
@@ -330,13 +355,26 @@
             halves[1] = True
         pack2[:, g * gw:(g + 1) * gw] = summed(g).astype(jnp.bfloat16)
         for p in range(members):
-            @pl.when(p != m)
+            @pl.when(abroad(p))
             def _(p=p, g=g):
                 two_copy(p, g).start()
+        two_copy(sibling, g).start()
         keep = pltpu.make_async_copy(
             pack2.at[:, pl.ds(g * gw, gw)], out2.at[:, cols(mine + g * gw, gw)],
             two_recv.at[m, g])
         keep.start()
+
+    for p in range(members):
+        @pl.when(abroad(p))
+        def _(p=p):
+            arrived(out1.at[:, pl.ds(p * core, core)], one_recv.at[p])
+            one_pass(p).start()
+    for g in inner_first:
+        for p in range(members):
+            @pl.when(abroad(p))
+            def _(p=p, g=g):
+                arrived(out2.at[:, pl.ds(p * core + g * gw, gw)], two_recv.at[p, g])
+                two_pass(p, g).start()
 
     for side in range(2):
         halo_copies[side].wait_send()
@@ -361,13 +399,43 @@
                 left_copy(p).wait_send()
             if p != last:
                 right_copy(p).wait_send()
+
+        @pl.when(abroad(p))
+        def _(p=p):
             one_copy(p).wait_send()
+            one_pass(p).wait_send()
             for g in range(groups):
                 two_copy(p, g).wait_send()
-    for i in range(members):
-        arrived(out1.at[:, pl.ds(i * core, core)], one_recv.at[i])
-        for g in range(groups):
-            arrived(out2.at[:, pl.ds(i * core + g * gw, gw)], two_recv.at[i, g])
+                two_pass(p, g).wait_send()
+
+        @pl.when(jnp.logical_not(abroad(p)))
+        def _(p=p):
+            arrived(out1.at[:, pl.ds(p * core, core)], one_recv.at[p])
+            for g in range(groups):
+                arrived(out2.at[:, pl.ds(p * core + g * gw, gw)], two_recv.at[p, g])
+    one_copy(sibling).wait_send()
+    for g in range(groups):
+        two_copy(sibling, g).wait_send()
+
+
+def widen(first, second, out1, out2, narrow, wide, read_sem, write_sem):
+    part = first.shape[1] // 3
+    reads, writes = [], []
+    for i, (source, out) in enumerate(((first, out1), (second, out2))):
+        for k in range(3):
+            at = pl.ds(k * part, part)
+            reads.append(pltpu.make_async_copy(
+                source.at[:, at], narrow.at[i, :, at], read_sem.at[i, k]))
+            writes.append(pltpu.make_async_copy(
+                wide.at[i, :, at], out.at[:, at], write_sem.at[i, k]))
+            reads[-1].start()
+    for n, (read, write) in enumerate(zip(reads, writes)):
+        i, at = n // 3, pl.ds(n % 3 * part, part)
+        read.wait()
+        wide[i, :, at] = narrow[i, :, at].astype(jnp.float32)
+        write.start()
+    for write in writes:
+        write.wait()
 
 
 def on_device(tiles, members, state, ensemble, vertical, coords, pairs, pair_count):
@@ -379,15 +447,17 @@
     core = nb * BLOCK
     width = core + 2 * HALO
     dma = pltpu.SemaphoreType.DMA
-    vmem = pl.BlockSpec(memory_space=pltpu.VMEM)
-    hbm = pl.BlockSpec(memory_space=pl.ANY)
+    hbm = pl.BlockSpec(memory_space=pltpu.HBM)
+    free = pl.BlockSpec(memory_space=pl.ANY)
     smem = pl.BlockSpec(memory_space=pltpu.SMEM)
     first, second = pl.pallas_call(
         functools.partial(kernel, tiles, members, blocks_dev, group),
         out_shape=[jax.ShapeDtypeStruct((levels, cols_dev), jnp.bfloat16)] * 2,
-        in_specs=[hbm, hbm, vmem, hbm, vmem, smem],
-        out_specs=[hbm, hbm],
+        in_specs=[hbm, hbm, hbm, hbm, hbm, smem],
+        out_specs=[free, free],
         scratch_shapes=[
+            pltpu.VMEM(vertical.shape, jnp.bfloat16),
+            pltpu.VMEM(pairs.shape, jnp.int32),
             pltpu.VMEM((members, levels, width), jnp.bfloat16),
             pltpu.VMEM((levels, width), jnp.float32),
             pltpu.VMEM((2, width), jnp.int32),
@@ -398,19 +468,31 @@
             pltpu.VMEM((2, levels, HALO), jnp.float32),
             pltpu.VMEM((levels, core), jnp.bfloat16),
             pltpu.VMEM((levels, core), jnp.bfloat16),
-            dma((2,)),
+            dma((4,)),
             dma((members,)), dma((members,)), dma((members,)),
             dma((members,)), dma((members,)), dma((members,)),
             dma((4,)), dma((4,)),
             dma((2,)), dma((2,)),
             dma((members,)), dma((members,)),
             dma((members, groups)), dma((members, groups)),
+            dma((members,)), dma((members, groups)),
         ],
         compiler_params=pltpu.CompilerParams(
-            collective_id=0, has_side_effects=True, vmem_limit_bytes=40 * 1024 * 1024
+            collective_id=0, has_side_effects=True, vmem_limit_bytes=60 * 1024 * 1024
         ),
     )(state, ensemble, vertical, coords, pairs, pair_count)
-    return first.astype(jnp.float32), second.astype(jnp.float32)
+    return pl.pallas_call(
+        widen,
+        out_shape=[jax.ShapeDtypeStruct((levels, cols_dev), jnp.float32)] * 2,
+        in_specs=[hbm, hbm],
+        out_specs=[hbm, hbm],
+        scratch_shapes=[
+            pltpu.VMEM((2, levels, cols_dev), jnp.bfloat16),
+            pltpu.VMEM((2, levels, cols_dev), jnp.float32),
+            dma((2, 3)), dma((2, 3)),
+        ],
+        compiler_params=pltpu.CompilerParams(vmem_limit_bytes=60 * 1024 * 1024),
+    )(first, second)
 
 
 def solution(mesh):

time: 32.5 us -> 27 us (0.83)
  the two profiles are of different devices: /device:TPU:0 before, /device:TPU:5 now
where the time goes in v2:
time: 27 us; the launch traced here: 26.9 us
  Pallas kernels  25.6 us (95%)
  between operations  1.29 us (5%)
    pallas_call x1, Pallas kernels, on_device(): pl.pallas_call(functools.partial(kernel, tiles, members, blocks_dev, grou...  23.4 us
    pallas_call x1, Pallas kernels, on_device(): pl.pallas_call(widen, out_shape=[jax.ShapeDtypeStruct((levels, cols_dev),...  2.16 us

profile of v2, /device:TPU:5, one launch (start us, length us, event | category | flops | bytes accessed | tf_op | source)
XLA Modules:
  0.0 26.9 jit_solution(4382705032342329086)
XLA Ops:
  1.3 23.4 %shard_map.77 = (bf16[32,6144]{1,0:T(8,128)(2,1)}, bf16[32,6144]{1,0:T(8,128)(2,1)}) custom-call(f32[32,6144]{1,0:T(8,128)} %state.1, bf16[1,32,6144]{2,1,0:T(8,128)(2,1)} %ens.1, bf16[32,32]{1,0:T(8,128)(2,1)} %vertical_in.1, s32[2,6144]{1,0:T(2,128)} %coords.1, s32[2,240]{1,0:T(2,128)} %pairs_in.1, s32[1]{0:T(128)S(6)} %copy.8.count), custom_call_target="tpu_custom_call" | custom-call | tf_op jit(solution)/shard_map/pallas_call | solution.py:453
  24.7 2.2 %shard_map.78 = (f32[32,6144]{1,0:T(8,128)}, f32[32,6144]{1,0:T(8,128)}) custom-call(bf16[32,6144]{1,0:T(8,128)(2,1)} %get-tuple-element.4.first, bf16[32,6144]{1,0:T(8,128)(2,1)} %get-tuple-element.5.second), custom_call_target="tpu_custom_call" | custom-call | tf_op jit(solution)/shard_map/pallas_call | solution.py:484

commit v3 on v2

--- a/solution.py
+++ b/solution.py
@@ -10,6 +10,12 @@
 BLOCK = 128
 REACH = 2
 SCALE = 4.0
+
+
+def CHUNKS(groups):
+    return [(1, groups - 2), (groups - 1, 1), (0, 1)] if groups > 2 else [(0, groups)]
+
+
 HALO = REACH * BLOCK
 FAR = 131072.0
 MESH = pl.DeviceIdType.MESH
@@ -81,38 +87,48 @@
         def _(p=p):
             pl.semaphore_signal(barrier, inc=1, device_id=(up, p), device_id_type=MESH)
 
+    def inside(p):
+        lo, hi = max(p * core - HALO, 0), min((p + 1) * core + HALO, cols_dev)
+        return pl.ds(lo, hi - lo), pl.ds(lo - (p * core - HALO), hi - lo)
+
+    reach = group + 2 * REACH
+    if group == REACH and ext > 2 * reach:
+        pieces = [(0, reach), (ext - reach, reach), (reach, ext - 2 * reach)]
+    else:
+        pieces = [(0, ext)]
+    early = len(pieces) - 1
+
+    def inside_piece(p, k):
+        start = p * core - HALO
+        lo = max(start + pieces[k][0] * BLOCK, 0)
+        hi = min(start + (pieces[k][0] + pieces[k][1]) * BLOCK, cols_dev)
+        return pl.ds(lo, hi - lo), pl.ds(lo - start, hi - lo)
+
     mine = m * core
     small = [
         pltpu.make_async_copy(pairs_in, pairs, local_sem.at[2]),
         pltpu.make_async_copy(vertical_in, vertical, local_sem.at[3]),
     ]
-    stay = [
-        pltpu.make_async_copy(
-            state.at[:, cols(mine, core)], field.at[:, core_x], local_sem.at[0]),
-        pltpu.make_async_copy(
-            coords.at[:, cols(mine, core)], xy.at[:, core_x], local_sem.at[1]),
-        pltpu.make_async_copy(
-            ens.at[0, :, cols(mine, core)], ensx.at[m, :, core_x], core_recv.at[m]),
-    ]
-    stay[1].start()
+
+    def stay(p):
+        there, here = inside(p)
+        return [
+            pltpu.make_async_copy(coords.at[:, there], xy.at[:, here], local_sem.at[1]),
+            pltpu.make_async_copy(state.at[:, there], field.at[:, here], local_sem.at[0]),
+        ] + [
+            pltpu.make_async_copy(
+                ens.at[0, :, inside_piece(p, k)[0]], ensx.at[m, :, inside_piece(p, k)[1]],
+                core_recv.at[m, k])
+            for k in range(len(pieces))
+        ]
+
+    for p in range(members):
+        @pl.when(p == m)
+        def _(p=p):
+            for copy in stay(p):
+                copy.start()
     for copy in small:
         copy.start()
-    stay[0].start()
-    stay[2].start()
-
-    @pl.when(m > 0)
-    def _():
-        at = cols(mine - HALO, HALO)
-        pltpu.make_async_copy(state.at[:, at], field.at[:, left_x], edge_recv.at[0]).start()
-        pltpu.make_async_copy(coords.at[:, at], xy.at[:, left_x], edge_recv.at[1]).start()
-        pltpu.make_async_copy(ens.at[0, :, at], ensx.at[m, :, left_x], left_recv.at[m]).start()
-
-    @pl.when(m < last)
-    def _():
-        at = cols(mine + core, HALO)
-        pltpu.make_async_copy(state.at[:, at], field.at[:, right_x], edge_recv.at[2]).start()
-        pltpu.make_async_copy(coords.at[:, at], xy.at[:, right_x], edge_recv.at[3]).start()
-        pltpu.make_async_copy(ens.at[0, :, at], ensx.at[m, :, right_x], right_recv.at[m]).start()
 
     dist = jnp.sqrt(iota((8, BLOCK), 1).astype(jnp.float32))
     table = gaspari(dist / SCALE).astype(jnp.bfloat16).astype(jnp.float32)
@@ -145,39 +161,23 @@
         for copy in edge_down:
             copy.start()
 
-    def core_copy(p):
+    def core_copy(p, k):
+        there, here = inside_piece(p, k)
         return remote(
-            ens.at[0, :, pl.ds(p * core, core)], ensx.at[m, :, core_x],
-            core_send.at[p], core_recv.at[m], (t, p))
-
-    def left_copy(p):
-        if p == 0:
-            return remote(
-                ens.at[0, :, high], ensx.at[m, :, left_x],
-                left_send.at[p], left_recv.at[m], (up, 0))
-        return remote(
-            ens.at[0, :, pl.ds(p * core - HALO, HALO)], ensx.at[m, :, left_x],
-            left_send.at[p], left_recv.at[m], (t, p))
-
-    def right_copy(p):
-        if p == last:
-            return remote(
-                ens.at[0, :, low], ensx.at[m, :, right_x],
-                right_send.at[p], right_recv.at[m], (down, last))
-        return remote(
-            ens.at[0, :, pl.ds((p + 1) * core, HALO)], ensx.at[m, :, right_x],
-            right_send.at[p], right_recv.at[m], (t, p))
-
-    left_copy(0).start()
-    right_copy(last).start()
-    for p in range(members):
-        @pl.when(p != m)
-        def _(p=p):
-            core_copy(p).start()
-            if p != 0:
-                left_copy(p).start()
-            if p != last:
-                right_copy(p).start()
+            ens.at[0, :, there], ensx.at[m, :, here],
+            core_send.at[p, k], core_recv.at[m, k], (t, p))
+
+    left_copy = remote(
+        ens.at[0, :, high], ensx.at[m, :, left_x], left_send.at[0], left_recv.at[m], (up, 0))
+    right_copy = remote(
+        ens.at[0, :, low], ensx.at[m, :, right_x], right_send.at[0], right_recv.at[m], (down, last))
+    left_copy.start()
+    right_copy.start()
+    for k in range(len(pieces)):
+        for p in range(members):
+            @pl.when(p != m)
+            def _(p=p, k=k):
+                core_copy(p, k).start()
 
     def arrived(ref, sem):
         pltpu.make_async_copy(ref, ref, sem).wait()
@@ -204,9 +204,19 @@
     same = iota((tall, tall), 0) // levels == iota((tall, tall), 1) // levels
     diagonal = jnp.where(same, stacked, 0.0).astype(jnp.bfloat16)
 
-    stay[1].wait()
-    arrived(xy.at[:, left_x], edge_recv.at[1])
-    arrived(xy.at[:, right_x], edge_recv.at[3])
+    for p in range(members):
+        @pl.when(p == m)
+        def _(p=p):
+            stay(p)[0].wait()
+
+    @pl.when(m == 0)
+    def _():
+        arrived(xy.at[:, left_x], edge_recv.at[1])
+
+    @pl.when(m == last)
+    def _():
+        arrived(xy.at[:, right_x], edge_recv.at[3])
+
     lane = iota((1, width), 1)
     block = lane >> 7
     rel = xy[0:1, :] - step * (t * blocks_dev + m * nb - REACH + block)
@@ -274,28 +284,62 @@
         + list(range(max(groups - edges, 0), groups))
         + list(range(groups))))
     inner_first = order[::-1]
-
-    stay[0].wait()
-    arrived(field.at[:, left_x], edge_recv.at[0])
-    arrived(field.at[:, right_x], edge_recv.at[2])
-    for i in range(members):
-        arrived(ensx.at[i, :, core_x], core_recv.at[i])
-        arrived(ensx.at[i, :, left_x], left_recv.at[i])
-        arrived(ensx.at[i, :, right_x], right_recv.at[i])
-    for e in range(0, ext, 2) if ext % 2 == 0 else range(ext):
-        size = 2 * BLOCK if ext % 2 == 0 else BLOCK
-        lift(e * BLOCK, size, field[:, e * BLOCK:e * BLOCK + size])
+    chunks = CHUNKS(groups)
+
+    def chunk(k):
+        return chunks[k][0] * gw, chunks[k][1] * gw
+
+
+    for p in range(members):
+        @pl.when(p == m)
+        def _(p=p):
+            arrived(field.at[:, inside(p)[1]], local_sem.at[0])
+
+    def piece_arrived(k):
+        for p in range(members):
+            @pl.when(p == m)
+            def _(p=p):
+                for i in range(members):
+                    arrived(ensx.at[i, :, inside_piece(p, k)[1]], core_recv.at[i, k])
+
+    def lift_piece(k):
+        start, many = pieces[k]
+        span = 2 if many % 2 == 0 else 1
+        for e in range(start, start + many, span):
+            at = e * BLOCK
+            lift(at, span * BLOCK, field[:, at:at + span * BLOCK])
+
+    for k in range(max(early, 1)):
+        piece_arrived(k)
+
+    @pl.when(m == 0)
+    def _():
+        arrived(field.at[:, left_x], edge_recv.at[0])
+        for i in range(members):
+            arrived(ensx.at[i, :, left_x], left_recv.at[i])
+
+    @pl.when(m == last)
+    def _():
+        arrived(field.at[:, right_x], edge_recv.at[2])
+        for i in range(members):
+            arrived(ensx.at[i, :, right_x], right_recv.at[i])
+
+    for k in range(max(early, 1)):
+        lift_piece(k)
 
     to_left = (jnp.where(m == 0, down, t), jnp.where(m == 0, last, m - 1))
     to_right = (jnp.where(m == last, up, t), jnp.where(m == last, 0, m + 1))
     halo_copies = [
-        remote(own1.at[:, pl.ds(0, HALO)], halo1.at[1], halo_send.at[0], halo_recv.at[1], to_left),
-        remote(own1.at[:, pl.ds(core - HALO, HALO)], halo1.at[0],
+        remote(pack1.at[:, pl.ds(0, HALO)], halo1.at[1], halo_send.at[0], halo_recv.at[1], to_left),
+        remote(pack1.at[:, pl.ds(core - HALO, HALO)], halo1.at[0],
                halo_send.at[1], halo_recv.at[0], to_right),
     ]
     sent = [False, False]
     done = set()
-    for g in order:
+    for n, g in enumerate(order):
+        if early and n == 2:
+            piece_arrived(early)
+            lift_piece(early)
         result = summed(g)
         own1[:, g * gw:(g + 1) * gw] = result
         pack1[:, g * gw:(g + 1) * gw] = result.astype(jnp.bfloat16)
@@ -313,24 +357,34 @@
     def one_copy(p):
         return remote(pack1, out1.at[:, own_cols], one_send.at[p], one_recv.at[m], (t, p))
 
-    def two_copy(p, g):
+    def two_copy(p, k):
+        at, size = chunk(k)
         return remote(
-            pack2.at[:, pl.ds(g * gw, gw)], out2.at[:, cols(mine + g * gw, gw)],
-            two_send.at[p, g], two_recv.at[m, g], (t, p))
+            pack2.at[:, pl.ds(at, size)], out2.at[:, cols(mine + at, size)],
+            two_send.at[p, k], two_recv.at[m, k], (t, p))
 
     sibling = m + 1 - 2 * lax.rem(m, 2)
 
     def abroad(p):
         return (p != m) & (lax.rem(m, 2) == p % 2)
+
+    def relayed(k):
+        return len(chunks) == 1 or k == 0
+
+    def reached(p, k):
+        return abroad(p) if relayed(k) else (p != m) & (p != sibling)
 
     def one_pass(p):
         at = pl.ds(p * core, core)
         return remote(out1.at[:, at], out1.at[:, at], one_fwd.at[p], one_recv.at[p], (t, sibling))
 
-    def two_pass(p, g):
-        at = pl.ds(p * core + g * gw, gw)
+    def two_at(p, k):
+        at, size = chunk(k)
+        return out2.at[:, pl.ds(p * core + at, size)]
+
+    def two_pass(p, k):
         return remote(
-            out2.at[:, at], out2.at[:, at], two_fwd.at[p, g], two_recv.at[p, g], (t, sibling))
+            two_at(p, k), two_at(p, k), two_fwd.at[p, k], two_recv.at[p, k], (t, sibling))
 
     for p in range(members):
         @pl.when(abroad(p))
@@ -343,38 +397,43 @@
     for g in range(groups):
         lift(HALO + g * gw, gw, own1[:, g * gw:(g + 1) * gw])
     halves = [False, False]
-    keep2 = []
+    ready, sent2 = set(), []
     for g in inner_first:
         if not halves[0] and g * gw < HALO:
             halo_copies[1].wait_recv()
-            lift(0, HALO, halo1[0])
+            lift(0, HALO, halo1[0].astype(jnp.float32))
             halves[0] = True
         if not halves[1] and (g + 1) * gw > core - HALO:
             halo_copies[0].wait_recv()
-            lift(HALO + core, HALO, halo1[1])
+            lift(HALO + core, HALO, halo1[1].astype(jnp.float32))
             halves[1] = True
         pack2[:, g * gw:(g + 1) * gw] = summed(g).astype(jnp.bfloat16)
+        ready.add(g)
+        for k, (start, many) in enumerate(chunks):
+            if k in sent2 or not set(range(start, start + many)) <= ready:
+                continue
+            sent2.append(k)
+            for p in range(members):
+                @pl.when(reached(p, k))
+                def _(p=p, k=k):
+                    two_copy(p, k).start()
+            two_copy(sibling, k).start()
+            at, size = chunk(k)
+            pltpu.make_async_copy(
+                pack2.at[:, pl.ds(at, size)], out2.at[:, cols(mine + at, size)],
+                two_recv.at[m, k]).start()
+
+    for p in range(members):
+        @pl.when(abroad(p))
+        def _(p=p):
+            arrived(out1.at[:, pl.ds(p * core, core)], one_recv.at[p])
+            one_pass(p).start()
+    for k in filter(relayed, sent2):
         for p in range(members):
             @pl.when(abroad(p))
-            def _(p=p, g=g):
-                two_copy(p, g).start()
-        two_copy(sibling, g).start()
-        keep = pltpu.make_async_copy(
-            pack2.at[:, pl.ds(g * gw, gw)], out2.at[:, cols(mine + g * gw, gw)],
-            two_recv.at[m, g])
-        keep.start()
-
-    for p in range(members):
-        @pl.when(abroad(p))
-        def _(p=p):
-            arrived(out1.at[:, pl.ds(p * core, core)], one_recv.at[p])
-            one_pass(p).start()
-    for g in inner_first:
-        for p in range(members):
-            @pl.when(abroad(p))
-            def _(p=p, g=g):
-                arrived(out2.at[:, pl.ds(p * core + g * gw, gw)], two_recv.at[p, g])
-                two_pass(p, g).start()
+            def _(p=p, k=k):
+                arrived(two_at(p, k), two_recv.at[p, k])
+                two_pass(p, k).start()
 
     for side in range(2):
         halo_copies[side].wait_send()
@@ -389,33 +448,37 @@
         for copy in edge_down:
             copy.wait_send()
 
-    left_copy(0).wait_send()
-    right_copy(last).wait_send()
+    left_copy.wait_send()
+    right_copy.wait_send()
     for p in range(members):
         @pl.when(p != m)
         def _(p=p):
-            core_copy(p).wait_send()
-            if p != 0:
-                left_copy(p).wait_send()
-            if p != last:
-                right_copy(p).wait_send()
+            for k in range(len(pieces)):
+                core_copy(p, k).wait_send()
 
         @pl.when(abroad(p))
         def _(p=p):
             one_copy(p).wait_send()
             one_pass(p).wait_send()
-            for g in range(groups):
-                two_copy(p, g).wait_send()
-                two_pass(p, g).wait_send()
+            for k in filter(relayed, sent2):
+                two_pass(p, k).wait_send()
 
         @pl.when(jnp.logical_not(abroad(p)))
         def _(p=p):
             arrived(out1.at[:, pl.ds(p * core, core)], one_recv.at[p])
-            for g in range(groups):
-                arrived(out2.at[:, pl.ds(p * core + g * gw, gw)], two_recv.at[p, g])
+            for k in filter(relayed, sent2):
+                arrived(two_at(p, k), two_recv.at[p, k])
+
+        for k in sent2:
+            @pl.when(reached(p, k))
+            def _(p=p, k=k):
+                two_copy(p, k).wait_send()
+
+            if not relayed(k):
+                arrived(two_at(p, k), two_recv.at[p, k])
     one_copy(sibling).wait_send()
-    for g in range(groups):
-        two_copy(sibling, g).wait_send()
+    for k in sent2:
+        two_copy(sibling, k).wait_send()
 
 
 def widen(first, second, out1, out2, narrow, wide, read_sem, write_sem):
@@ -465,12 +528,12 @@
             pltpu.VMEM((groups, (group + 2 * REACH) * BLOCK, group * BLOCK), jnp.bfloat16),
             pltpu.VMEM((members * levels, width), jnp.bfloat16),
             pltpu.VMEM((levels, core), jnp.float32),
-            pltpu.VMEM((2, levels, HALO), jnp.float32),
+            pltpu.VMEM((2, levels, HALO), jnp.bfloat16),
             pltpu.VMEM((levels, core), jnp.bfloat16),
             pltpu.VMEM((levels, core), jnp.bfloat16),
             dma((4,)),
-            dma((members,)), dma((members,)), dma((members,)),
-            dma((members,)), dma((members,)), dma((members,)),
+            dma((members, 3)), dma((members,)), dma((members,)),
+            dma((members, 3)), dma((members,)), dma((members,)),
             dma((4,)), dma((4,)),
             dma((2,)), dma((2,)),
             dma((members,)), dma((members,)),

time: 27 us -> 26.4 us (0.978)
  the two profiles are of different devices: /device:TPU:5 before, /device:TPU:0 now
where the time goes in v3:
time: 26.4 us; the launch traced here: 26.3 us
  Pallas kernels  25 us (95%)
  between operations  1.29 us (5%)
    pallas_call x1, Pallas kernels, on_device(): pl.pallas_call(functools.partial(kernel, tiles, members, blocks_dev, grou...  22.8 us
    pallas_call x1, Pallas kernels, on_device(): pl.pallas_call(widen, out_shape=[jax.ShapeDtypeStruct((levels, cols_dev),...  2.16 us

profile of v3, /device:TPU:0, one launch (start us, length us, event | category | flops | bytes accessed | tf_op | source)
XLA Modules:
  0.0 26.3 jit_solution(4058018907874919717)
XLA Ops:
  1.3 22.8 %shard_map.77 = (bf16[32,6144]{1,0:T(8,128)(2,1)}, bf16[32,6144]{1,0:T(8,128)(2,1)}) custom-call(f32[32,6144]{1,0:T(8,128)} %state.1, bf16[1,32,6144]{2,1,0:T(8,128)(2,1)} %ens.1, bf16[32,32]{1,0:T(8,128)(2,1)} %vertical_in.1, s32[2,6144]{1,0:T(2,128)} %coords.1, s32[2,240]{1,0:T(2,128)} %pairs_in.1, s32[1]{0:T(128)S(6)} %copy.8.count), custom_call_target="tpu_custom_call" | custom-call | tf_op jit(solution)/shard_map/pallas_call | solution.py:516
  24.1 2.2 %shard_map.78 = (f32[32,6144]{1,0:T(8,128)}, f32[32,6144]{1,0:T(8,128)}) custom-call(bf16[32,6144]{1,0:T(8,128)(2,1)} %get-tuple-element.4.first, bf16[32,6144]{1,0:T(8,128)(2,1)} %get-tuple-element.5.second), custom_call_target="tpu_custom_call" | custom-call | tf_op jit(solution)/shard_map/pallas_call | solution.py:547
